TPU v7x, 128 devices: a whole 4x4x4 slice. The times are simulated.
128 devices in a mesh: leaf: 32 (over x, y, core), sub: 4 (over z).
Axes of the slice: x: 4, y: 4, z: 4, core: 2. Of those that a mesh axis runs over, the one named last changes fastest.
Arguments:
- right_sides: float32 [16, 128, 1024], P(None, 'leaf', 'sub'), may hold values from -6 to 6
- leaf_order: int32 [128, 1024], P('leaf'), may hold values from 0 to 1023, each once within a row
- leaf_inverse: float32 [128, 1024, 1024], P('leaf', 'sub'), may hold values from -1 to 3
- left_basis: float32 [7, 64, 128, 1024], P(None, None, 'leaf', 'sub'), may hold values from -0.375 to 0.375
- column_factor_bases: float32 [7, 64, 128, 1024], P(None, None, 'leaf', 'sub'), may hold values from -6 to 6
- core_inverse: float32 [128, 128, 128], P('leaf'), may hold values from -1 to 2
Outputs:
- solution: float32 [16, 128, 1024], P(None, 'leaf', 'sub')
Inputs may be any that keep to these rules, and one draw needn't show every extreme that they name: `leaf_order`: each row holds every number of 0 to 1023 once.
All inputs are finite; a program needn't handle non-finite values.
Results may differ from a plain program's by a relative error of at most 0.0001.
Values sent between devices are 32-bit elements; how exact they have to be, the bound alone decides.
A program may use at most 64 MiB of HBM per device.

v0:
```python
import math

import jax
import jax.numpy as jnp
from jax import lax
from jax.sharding import PartitionSpec as P

exact_precision = lax.Precision.HIGHEST


def per_device(
    right_sides, leaf_order, leaf_inverse, left_basis, column_factor_bases, core_inverse
):
    members, local_leaves, leaf_part = right_sides.shape
    leaf_size = leaf_order.shape[1]
    levels = left_basis.shape[0]
    rank_count = left_basis.shape[1]
    upper_count = lax.axis_size("leaf").bit_length() - 1
    lower_count = levels - upper_count
    leaf_index = lax.axis_index("leaf")
    gathered = lax.all_gather(right_sides, "sub", axis=2, tiled=True)
    positions = jnp.arange(leaf_size, dtype=jnp.int32)
    selection = (leaf_order[:, :, None] == positions[None, None, :]).astype(jnp.float32)
    ordered = jnp.einsum("ljk,mlk->mlj", selection, gathered, precision=exact_precision)
    iterate = jnp.einsum("lij,mlj->mli", leaf_inverse, ordered, precision=exact_precision)
    all_cores = lax.all_gather(core_inverse, "leaf", axis=0, tiled=True)
    for depth in range(1, lower_count + 1):
        node_span = 2**depth
        half_span = node_span // 2
        groups = local_leaves // node_span
        norm_factor = 1.0 / math.sqrt(leaf_size * half_span)
        vectors = column_factor_bases[depth - 1].reshape(
            rank_count, groups, 2, half_span * leaf_part
        )
        blocks = iterate.reshape(members, groups, 2, half_span * leaf_part)
        projected_values = (
            jnp.einsum("rghp,mghp->gmhr", vectors, blocks, precision=exact_precision) * norm_factor
        )
        projected_values = projected_values.reshape(groups, members, 2 * rank_count)
        projected_values = lax.psum(projected_values, "sub")
        coupling_block = core_inverse.reshape(groups, node_span, 2 * rank_count, 2 * rank_count)[
            :, half_span - 1
        ]
        solved_rows = jnp.einsum(
            "jyi,jvi->jvy", coupling_block, projected_values, precision=exact_precision
        )
        solved_rows = solved_rows.reshape(groups, members, 2, rank_count)
        bases_up = left_basis[depth - 1].reshape(rank_count, groups, 2, half_span * leaf_part)
        update = jnp.einsum("rghp,gmhr->mghp", bases_up, solved_rows, precision=exact_precision)
        iterate = iterate - update.reshape(members, local_leaves, leaf_part)
    for depth in range(lower_count + 1, levels + 1):
        stride = 2 ** (depth - lower_count)
        half_dev = stride // 2
        node_index = leaf_index // stride
        which_half = leaf_index // half_dev % 2
        groups = lax.axis_size("leaf") // stride
        selector = (jnp.arange(groups, dtype=jnp.int32) == node_index).astype(jnp.float32)
        norm_factor = 1.0 / math.sqrt(leaf_size * local_leaves * half_dev)
        partial_value = (
            jnp.einsum(
                "rlp,mlp->mr", column_factor_bases[depth - 1], iterate, precision=exact_precision
            )
            * norm_factor
        )
        empty_half = jnp.zeros_like(partial_value)
        positioned_rows = jnp.where(
            which_half == 0,
            jnp.concatenate([partial_value, empty_half], 1),
            jnp.concatenate([empty_half, partial_value], 1),
        )
        summed = lax.psum(selector[:, None, None] * positioned_rows[None], ("leaf", "sub"))
        stacked_rows = lax.dynamic_index_in_dim(summed, node_index, 0, keepdims=False)
        slot_index = (node_index * stride + half_dev) * local_leaves - 1
        coupling_block = lax.dynamic_index_in_dim(all_cores, slot_index, 0, keepdims=False)
        solved_rows = jnp.dot(stacked_rows, coupling_block.T, precision=exact_precision)
        own_solved = lax.dynamic_slice_in_dim(solved_rows, which_half * rank_count, rank_count, 1)
        iterate = iterate - jnp.einsum(
            "rlp,mr->mlp", left_basis[depth - 1], own_solved, precision=exact_precision
        )
    return iterate


def solution(mesh):
    in_specs = (
        P(None, "leaf", "sub"),
        P("leaf", None),
        P("leaf", "sub", None),
        P(None, None, "leaf", "sub"),
        P(None, None, "leaf", "sub"),
        P("leaf", None, None),
    )
    out_specs = P(None, "leaf", "sub")
    return jax.shard_map(
        per_device, mesh=mesh, in_specs=in_specs, out_specs=out_specs, check_vma=False
    )
```

profile of v0, /device:TPU:1, one launch (start us, length us, event | category | flops | bytes accessed | tf_op | source)
XLA Modules:
  0.0 566.0 jit_solution(7190398936195232060)
XLA Ops:
  7.4 2.7 fusion.61
  10.2 1.0 copy.44
  11.2 12.3 %all_gather.6 = f32[16,4,1024]{2,0,1:T(8,128)S(1)} all-gather(f32[16,4,256]{2,0,1:T(8,128)S(1)} %copy.44), channel_id=1, replica_groups=mesh['leaf'=32,'sub'=4] {'sub'}, dimensions={2}, use_global_device_ids=true | all-gather | bytes 327680 | tf_op jit(solution)/shard_map/all_gather | solution.py:21
  23.5 8.8 %fusion.2 = f32[16,4,1024]{2,0,1:T(8,128)S(1)} fusion(f32[16,4,1024]{2,0,1:T(8,128)S(1)} %all_gather.6, s32[4,1024]{1,0:T(4,128)} %param.7), kind=kOutput, calls=%fused_computation.3 | convolution fusion | flops 809500672 | bytes 540672 | tf_op jit(solution)/shard_map/ljk,mlk->mlj/dot_general | solution.py:24
  32.3 3.6 fusion.63
  36.4 12.3 %psum.49 = f32[2,16,128]{2,1,0:T(8,128)S(1)} all-reduce(f32[2,16,128]{2,1,0:T(8,128)S(1)} %reshape.91), channel_id=1, replica_groups=mesh['leaf'=32,'sub'=4] {'sub'}, use_global_device_ids=true, to_apply=%region_0.0 | all-reduce | flops 4096 | bytes 32768 | tf_op jit(solution)/shard_map/psum | solution.py:40
  49.1 1.1 fusion.62
  50.6 1.2 reshape.96
  51.8 0.3 fusion.4
  52.3 6.1 %psum.50 = f32[16,128]{1,0:T(8,128)S(1)} all-reduce(f32[16,128]{1,0:T(8,128)S(1)} %reshape.98), channel_id=1, replica_groups=mesh['leaf'=32,'sub'=4] {'sub'}, use_global_device_ids=true, to_apply=%region_1.0 | all-reduce | flops 2048 | bytes 16384 | tf_op jit(solution)/shard_map/psum | solution.py:40
  58.4 0.8 slice.65
  59.2 1.2 reshape.100
  61.1 1.2 fusion.9
  62.5 0.8 broadcast_multiply_fusion
  63.3 0.5 all-gather.2.cloned.1.call-update
  64.0 155.3 %all-reduce.13.cloned.1.call-done = f32[16,16,128]{2,1,0:T(8,128)} async-done(((f32[16,16,128]{2,1,0:T(8,128)}), f32[16,16,128]{2,1,0:T(8,128)}) %all-reduce.13.cloned.1.call-update) | async-done | bytes 131088 | tf_op jit(solution)/shard_map/psum | solution.py:71
  219.3 1.0 fusion.21
  220.3 1.3 convolution_subtract_fusion.4
  221.6 1.2 fusion.8
  223.0 0.7 broadcast_multiply_fusion.1
  223.9 136.2 %all-reduce.15.cloned.1.call-done = f32[8,16,128]{2,1,0:T(8,128)} async-done(((f32[8,16,128]{2,1,0:T(8,128)}), f32[8,16,128]{2,1,0:T(8,128)}) %all-reduce.15.cloned.1.call-update) | async-done | bytes 65552 | tf_op jit(solution)/shard_map/psum | solution.py:71
  360.0 1.0 fusion.19
  361.1 0.3 convolution_subtract_fusion.3
  361.4 1.2 fusion.7
  362.8 63.3 %psum.53 = f32[4,16,128]{2,1,0:T(8,128)S(1)} all-reduce(f32[4,16,128]{2,1,0:T(8,128)S(1)} %broadcast_multiply_fusion.2), channel_id=1, replica_groups=mesh['leaf'=32,'sub'=4] {'leaf','sub'}, use_global_device_ids=true, to_apply=%region_4.5 | all-reduce | flops 8192 | bytes 65536 | tf_op jit(solution)/shard_map/psum | solution.py:71
  426.2 1.0 fusion.17
  427.2 0.3 convolution_subtract_fusion.2
  428.0 63.1 %psum.54 = f32[2,16,128]{2,1,0:T(8,128)S(1)} all-reduce(f32[2,16,128]{2,1,0:T(8,128)S(1)} %broadcast_multiply_fusion.3), channel_id=1, replica_groups=mesh['leaf'=32,'sub'=4] {'leaf','sub'}, use_global_device_ids=true, to_apply=%region_5.6 | all-reduce | flops 4096 | bytes 32768 | tf_op jit(solution)/shard_map/psum | solution.py:71
  491.0 1.0 fusion.15
  492.8 63.7 %psum.55 = f32[16,128]{1,0:T(8,128)S(1)} all-reduce(f32[16,128]{1,0:T(8,128)S(1)} %select_multiply_fusion), channel_id=1, replica_groups=mesh['leaf'=32,'sub'=4] {'leaf','sub'}, use_global_device_ids=true, to_apply=%region_6.7 | all-reduce | flops 2048 | bytes 16384 | tf_op jit(solution)/shard_map/psum | solution.py:71
  556.6 1.0 fusion.13
  557.9 0.7 copy.67
  (44 shorter events, 4.2 us)
Async XLA Ops:
  7.4 211.9 %all-reduce.13.cloned.1.call-start = ((), (), s32[]{:S(2)}) async-start(), calls=%async_computation | async-start | bytes 262144 | tf_op jit(solution)/shard_map/psum | solution.py:71
  7.4 24.9 %copy-start = (f32[4,256,1024]{2,1,0:T(8,128)S(1)}, f32[4,256,1024]{2,1,0:T(8,128)}, u32[]{:S(2)}) copy-start(f32[4,256,1024]{2,1,0:T(8,128)} %param.8) | copy-start | bytes 12582916
  10.1 38.5 %copy-start.2 = (f32[4,128,128]{2,1,0:T(8,128)S(1)}, f32[4,128,128]{2,1,0:T(8,128)}, u32[]{:S(2)}) copy-start(f32[4,128,128]{2,1,0:T(8,128)} %param.11) | copy-start | bytes 786436
  10.2 38.9 %copy-start.1 = (f32[7,64,4,256]{3,2,1,0:T(4,128)S(1)}, f32[7,64,4,256]{3,2,1,0:T(4,128)}, u32[]{:S(2)}) copy-start(f32[7,64,4,256]{3,2,1,0:T(4,128)} %param.9) | copy-start | bytes 5505028
  63.2 156.1 %all-gather.2.cloned.1.call-start = ((), (), s32[]{:S(2)}) async-start(), calls=%async_computation.1 | async-start | bytes 8650752 | tf_op jit(solution)/shard_map/all_gather | solution.py:26
  63.8 296.2 %all-reduce.15.cloned.1.call-start = ((), (), s32[]{:S(2)}) async-start(), calls=%async_computation.2 | async-start | bytes 131072 | tf_op jit(solution)/shard_map/psum | solution.py:71
Sparse Core Ops, SparseCore 0:
  63.4 155.9 all-reduce.12
  224.8 135.2 all-reduce.14
Sparse Core Ops, SparseCore 1:
  66.0 62.4 all-gather.1
where the time goes:
time: 567 us; the launch traced here: 566 us
  waiting for transfers between devices  292 us (51%)
  blocking collectives  221 us (39%)
  matrix products  26.1 us (5%)
  between operations  15.3 us (3%)
  local copies, waits for them, and re-layouts  9.41 us (2%)
    psum x2, waiting for transfers between devices, per_device(): lax.psum(selector[:, None, None] * positioned_rows[None], ('leaf', 'sub'))  292 us
    psum x3, blocking collectives, per_device(): lax.psum(selector[:, None, None] * positioned_rows[None], ('leaf', 'sub'))  190 us
    psum x2, blocking collectives, per_device(): projected_values = lax.psum(projected_values, 'sub')  18.4 us
    all_gather x1, blocking collectives, per_device(): gathered = lax.all_gather(right_sides, 'sub', axis=2, tiled=True)  12.3 us
  transfers between devices with their start and end apart: 3, of which 2 were waited for; matrix products, arithmetic and copies ran while one was open for 0% of the time, Pallas kernels for 0%

commit v1 on v0

v1 whole, which is shorter than its diff:
```python
import math

import jax
import jax.numpy as jnp
from jax import lax
from jax.experimental import pallas as pl
from jax.experimental.pallas import tpu as pltpu
from jax.sharding import PartitionSpec as P

MESH = pl.DeviceIdType.MESH
f32, bf16 = jnp.float32, jnp.bfloat16

SLOT_LEVELS = (4, 5, 6, 7, 3, 2, 1)
COPIES = 96


def split(value):
    high = value.astype(bf16)
    return high, (value - high.astype(f32)).astype(bf16)


def nt(a, b):
    return lax.dot_general(a, b, (((1,), (1,)), ((), ())), preferred_element_type=f32)


def nn(a, b):
    return lax.dot_general(a, b, (((1,), (0,)), ((), ())), preferred_element_type=f32)


def product(dot, a, b_high, b_low):
    rows = a.shape[0]
    a_high, a_low = split(a)
    both = dot(jnp.concatenate([a_high, a_low], 0), b_high)
    return both[:rows] + both[rows:] + dot(a_high, b_low)


def apply_rows(a, matrix):
    return product(nt, a, *split(matrix))


def kernel(
    right, order, inverse, left, column, cores,
    out,
    rhs, index, inv, u32, v32, core,
    uh, ul, vh, vl,
    q1, q1h, q1l, q3, g21p, g21, rs, g3, ys, g45p, g45, xs, g6p, g6, g3p, ysp, xsp,
    xc, cb, c3,
    field, r1p, r1, r2p, r2, r3p, r3, r4p, r4,
    load_sem, send_sem, recv_sem, c_send, c_recv,
):
    members, leaves, part = right.shape
    leaf, z = lax.axis_index("leaf"), lax.axis_index("sub")
    c = lax.rem(leaf, 2)
    y = lax.rem(lax.div(leaf, 2), 4)
    x = lax.div(leaf, 8)
    me = 2 * z + c
    sibling = (leaf + 1 - 2 * c, z)
    z_peers = [(leaf, lax.rem(z + d, 4)) for d in (1, 2, 3)]
    zc_peers = [(leaf, lax.rem(z + d, 4)) for d in (1, 2, 3)]
    zc_peers += [(leaf + 1 - 2 * c, lax.rem(z + d, 4)) for d in (0, 1, 2, 3)]
    zc_index = [2 * lax.rem(z + d, 4) + c for d in (1, 2, 3)]
    zc_index += [2 * lax.rem(z + d, 4) + 1 - c for d in (0, 1, 2, 3)]
    y_peers = [(8 * x + 2 * lax.rem(y + d, 4) + c, z) for d in (1, 2, 3)]
    x_peers = [(8 * lax.rem(x + d, 4) + 2 * y + c, z) for d in (1, 2, 3)]

    count = [0]
    started = []

    def send(src, dst, device):
        i = count[0]
        count[0] += 1
        copy = pltpu.make_async_remote_copy(
            src_ref=src, dst_ref=dst, send_sem=send_sem.at[i], recv_sem=recv_sem.at[i],
            device_id=device, device_id_type=MESH,
        )
        copy.start()
        started.append(copy)
        return copy

    def receive(copies):
        for copy in copies:
            copy.wait_recv()

    loads = []

    def load(src, dst):
        copy = pltpu.make_async_copy(src, dst, load_sem.at[len(loads)])
        copy.start()
        loads.append(copy)
        return copy

    rhs_loads = [load(right.at[:, l, :], rhs.at[z, l]) for l in range(leaves)]
    order_load = load(order, index)
    basis_loads = [load(column.at[:, :, l, :], v32.at[l]) for l in range(leaves)]
    basis_loads += [load(left.at[:, :, l, :], u32.at[l]) for l in range(leaves)]
    core_load = load(cores, core)
    inverse_loads = [load(inverse.at[l], inv.at[l]) for l in range(leaves)]

    barrier = pltpu.get_barrier_semaphore()
    peers = zc_peers + y_peers + x_peers
    for peer in peers:
        pl.semaphore_signal(barrier, inc=1, device_id=peer, device_id_type=MESH)

    for copy in basis_loads:
        copy.wait()
    for l in range(leaves):
        for slot, level in enumerate(SLOT_LEVELS):
            norm = 1.0 / math.sqrt(1024 * 2 ** (level - 1))
            vh[l, slot], vl[l, slot] = split(v32[l, level - 1] * norm)
        for k in range(7):
            uh[l, k], ul[l, k] = split(u32[l, k])

    def gram(l, slots, levels):
        a_high, a_low = (t[l, slots[0]:slots[1]].reshape(-1, part) for t in (vh, vl))
        b_high, b_low = (t[l, levels[0]:levels[1]].reshape(-1, part) for t in (uh, ul))
        return nt(a_high, b_high) + nt(a_low, b_high) + nt(a_high, b_low)

    low_lanes = lax.broadcasted_iota(jnp.int32, (1, 128), 1) < 64

    def turn(a):
        return pltpu.roll(a, 64, a.ndim - 1)

    def low_low(a, b):
        return jnp.where(low_lanes, a, turn(b))

    def high_high(a, b):
        return jnp.where(low_lanes, turn(a), b)

    for l in range(leaves):
        block = gram(l, (0, 6), (0, 2))
        q1[:, 128 * l : 128 * l + 128] = block
        q1h[:, 128 * l : 128 * l + 128], q1l[:, 128 * l : 128 * l + 128] = split(block)
    for n in range(2):
        g21p[n] = low_low(q1[320:384, 256 * n : 256 * n + 128], q1[320:384, 256 * n + 128 : 256 * n + 256])

    for copy in rhs_loads:
        copy.wait()
    core_load.wait()
    pl.semaphore_wait(barrier, len(peers))
    rhs_copies = [[send(rhs.at[z, l], rhs.at[z, l], peer) for peer in z_peers] for l in range(leaves)]

    last_column = lax.rem(leaf, 8) == 7

    def c_copy(i, j, src, dst, device):
        return pltpu.make_async_remote_copy(
            src_ref=src, dst_ref=dst, send_sem=c_send.at[i], recv_sem=c_recv.at[j],
            device_id=device, device_id_type=MESH,
        )

    along_x = [c_copy(d, d, core.at[3], xc.at[x], x_peers[d]) for d in range(3)]
    along_y_one = [c_copy(3 + d, 3 + y, core.at[3], cb.at[y], y_peers[d]) for d in range(3)]
    along_y_three = [c_copy(6 + d, 6, xc.at[pl.ds(0, 3)], cb.at[pl.ds(3, 3)], y_peers[d]) for d in range(3)]
    to_sibling = c_copy(9, 7, cb, cb, sibling)
    third = c_copy(10, 8, core.at[3], c3, sibling)

    @pl.when(last_column)
    def _():
        for copy in along_x:
            copy.start()
        xc[x] = core[3]

    @pl.when(c == 0)
    def _():
        third.start()
        c3[...] = core[3]

    total = None
    for l in range(leaves):
        block = gram(l, (0, 4), (2, 6))
        total = block if total is None else total + block
    q3[...] = total.reshape(4, 8, 8, 256)
    rs[me] = q3[:, me]
    g21[z] = g21p[...]
    order_load.wait()
    for copy in inverse_loads:
        copy.wait()
    g21_copies = [send(g21p, g21.at[z], peer) for peer in z_peers]
    rs_copies = [send(q3.at[:, i], rs.at[me], peer) for i, peer in zip(zc_index, zc_peers, strict=True)]

    r1_copies = []
    for l in range(leaves):
        receive(rhs_copies[l])
        pieces = []
        for u in range(8):
            place = index[l : l + 1, 128 * u : 128 * u + 128]
            lane = jnp.broadcast_to(place & 127, (members, 128))
            tile = jnp.broadcast_to(place >> 7, (members, 128))
            piece = jnp.zeros((members, 128), f32)
            for t in range(8):
                source = rhs[t // 2, l, :, 128 * (t % 2) : 128 * (t % 2) + 128]
                piece = jnp.where(tile == t, jnp.take_along_axis(source, lane, axis=1), piece)
            pieces.append(piece)
        ordered = jnp.concatenate(pieces, 1)
        values = apply_rows(ordered, inv[l])
        field[l] = values
        r1p[l] = product(nt, values, vh[l, 5:7].reshape(128, part), vl[l, 5:7].reshape(128, part))
        if l % 2 == 1:
            pair = pl.ds(l - 1, 2)
            r1_copies += [send(r1p.at[pair], r1.at[z, pair], peer) for peer in z_peers]
    r1[z] = r1p[...]

    raw = None
    for l in range(leaves):
        block = product(nt, field[l], vh[l, 0:6].reshape(384, part), vl[l, 0:6].reshape(384, part))
        raw = block if raw is None else raw + block

    @pl.when(last_column)
    def _():
        for copy in along_x:
            copy.wait_recv()
        for copy in along_y_three:
            copy.start()
        cb[3:6] = xc[0:3]

    @pl.when(c == 1)
    def _():
        @pl.when(y < 3)
        def _():
            for copy in along_y_one:
                copy.start()
            cb[y] = core[3]

    receive(rs_copies)
    sum_a = rs[0] + rs[2] + rs[4] + rs[6]
    sum_b = rs[1] + rs[3] + rs[5] + rs[7]
    g3p[...] = low_low(sum_a[:, :, :128], sum_b[:, :, :128])
    g3[:, me] = g3p[...]
    ysp[...] = sum_a + sum_b
    ys[y] = ysp[...]
    g3_copies = [send(g3p, g3.at[:, me], peer) for peer in zc_peers]
    ys_copies = [send(ysp, ys.at[y], peer) for peer in y_peers]
    receive(g21_copies)
    coupling = g21[0] + g21[1] + g21[2] + g21[3]
    zeros = jnp.zeros((64, 128), f32)
    coupling = jnp.concatenate(
        [jnp.concatenate([coupling[0], zeros], 1), jnp.concatenate([zeros, coupling[1]], 1)], 0
    )

    receive(r1_copies)
    s = [r1[0, l] + r1[1, l] + r1[2, l] + r1[3, l] for l in range(leaves)]
    s1 = [apply_rows(high_high(s[2 * n], s[2 * n + 1]), core[2 * n]) for n in range(2)]
    p2 = low_low(s[0] + s[1], s[2] + s[3]) - apply_rows(jnp.concatenate(s1, 1), coupling)
    s2 = apply_rows(p2, core[1])
    own = [
        low_low(s1[0], s2),
        jnp.where(low_lanes, turn(s1[0]), turn(s2)),
        jnp.where(low_lanes, s1[1], s2),
        high_high(s1[1], s2),
    ]
    r2p[...] = raw - product(nt, jnp.concatenate(own, 1), q1h[...], q1l[...])
    r2_copies = [send(r2p, r2.at[me], peer) for peer in zc_peers]
    r2[me] = r2p[...]

    def correct(l, coefficients, levels):
        b_high, b_low = (t[l, levels[0]:levels[1]].reshape(-1, part) for t in (uh, ul))
        return product(nn, coefficients, b_high, b_low)

    for l in range(leaves):
        field[l] = field[l] - correct(l, own[l], (0, 2))

    @pl.when(c == 1)
    def _():
        for j in range(3):
            @pl.when(y != j)
            def _():
                c_copy(3, 3 + j, core.at[3], cb.at[j], sibling).wait_recv()

        @pl.when(y != 3)
        def _():
            along_y_three[0].wait_recv()

        to_sibling.start()

    receive(ys_copies)
    for n in range(2):
        g45p[4 * n : 4 * n + 4] = high_high(ys[2 * n, :, :, :128], ys[2 * n + 1, :, :, :128])
    halves = [ys[0, 2:4, :, 128:] + ys[1, 2:4, :, 128:], ys[2, 2:4, :, 128:] + ys[3, 2:4, :, 128:]]
    g45p[8:10] = low_low(halves[0], halves[1])
    xsp[...] = halves[0][1] + halves[1][1]
    g45[:, me] = g45p[...]
    xs[x] = xsp[...]
    xs_copies = [send(xsp, xs.at[x], peer) for peer in x_peers]
    g45_copies = [send(g45p, g45.at[:, me], peer) for peer in zc_peers]

    receive(g3_copies)

    @pl.when(c == 1)
    def _():
        third.wait_recv()

    receive(r2_copies)
    p_a = r2[0] + r2[2] + r2[4] + r2[6]
    p_b = r2[1] + r2[3] + r2[5] + r2[7]
    s3 = apply_rows(low_low(p_a[:, 256:], p_b[:, 256:]), c3[...])
    r3p[...] = p_a[:, :256] + p_b[:, :256] - apply_rows(s3, g3[...].reshape(256, 128))
    r3_copies = [send(r3p, r3.at[y], peer) for peer in y_peers]
    r3[y] = r3p[...]

    receive(xs_copies)
    for n in range(2):
        g6p[n] = high_high(xs[2 * n], xs[2 * n + 1])
    g6[:, me] = g6p[...]
    g6_copies = [send(g6p, g6.at[:, me], peer) for peer in zc_peers]

    @pl.when(c == 0)
    def _():
        to_sibling.wait_recv()

    receive(g45_copies)
    receive(r3_copies)
    s4, below = [], []
    for n in range(2):
        p4 = low_low(r3[2 * n, :, :128], r3[2 * n + 1, :, :128])
        s4.append(apply_rows(p4, cb[2 * n]))
        below.append(r3[2 * n] + r3[2 * n + 1] - apply_rows(s4[n], g45[4 * n : 4 * n + 4].reshape(256, 128)))
    s5 = apply_rows(high_high(below[0][:, :128], below[1][:, :128]), cb[1])
    r4p[...] = below[0][:, 128:] + below[1][:, 128:] - apply_rows(s5, g45[8:10].reshape(128, 128))
    r4_copies = [send(r4p, r4.at[x], peer) for peer in x_peers]
    r4[x] = r4p[...]

    own3 = jnp.where(c == 0, s3, turn(s3))
    own4 = jnp.where(y < 2, s4[0], s4[1])
    own4 = jnp.where(lax.rem(y, 2) == 1, own4, turn(own4))
    own5 = jnp.where(y < 2, s5, turn(s5))
    own34 = jnp.where(low_lanes, own3, own4)
    for l in range(leaves):
        field[l] = field[l] - correct(l, own34, (2, 4)) - correct(l, own5[:, :64], (4, 5))

    receive(g6_copies)
    coupling = jnp.concatenate(
        [
            jnp.concatenate([g6[0].reshape(64, 128), zeros], 1),
            jnp.concatenate([zeros, g6[1].reshape(64, 128)], 1),
        ],
        0,
    )
    receive(r4_copies)
    s6 = [apply_rows(low_low(r4[2 * n], r4[2 * n + 1]), cb[3 + 2 * n]) for n in range(2)]
    p7 = high_high(r4[0] + r4[1], r4[2] + r4[3]) - apply_rows(jnp.concatenate(s6, 1), coupling)
    s7 = apply_rows(p7, cb[4])
    own6 = jnp.where(x < 2, s6[0], s6[1])
    own6 = jnp.where(lax.rem(x, 2) == 0, own6, turn(own6))
    own7 = jnp.where(x < 2, turn(s7), s7)
    own67 = jnp.where(low_lanes, own6, own7)
    for l in range(leaves):
        out[l] = field[l] - correct(l, own67, (5, 7))

    for copy in started:
        copy.wait_send()

    @pl.when(last_column)
    def _():
        for copy in along_x + along_y_three:
            copy.wait_send()

    @pl.when(c == 1)
    def _():
        to_sibling.wait_send()

        @pl.when(y < 3)
        def _():
            for copy in along_y_one:
                copy.wait_send()

    @pl.when(c == 0)
    def _():
        third.wait_send()


def per_device(*inputs):
    members, leaves, part = inputs[0].shape
    size = 4 * part
    vmem = pltpu.VMEM
    scratch = [
        vmem((4, leaves, members, part), f32),
        vmem((leaves, size), jnp.int32),
        vmem((leaves, part, size), f32),
        vmem((leaves, 7, 64, part), f32),
        vmem((leaves, 7, 64, part), f32),
        vmem((leaves, 128, 128), f32),
        vmem((leaves, 7, 64, part), bf16),
        vmem((leaves, 7, 64, part), bf16),
        vmem((leaves, 7, 64, part), bf16),
        vmem((leaves, 7, 64, part), bf16),
        vmem((384, 512), f32),
        vmem((384, 512), bf16),
        vmem((384, 512), bf16),
        vmem((4, 8, 8, 256), f32),
        vmem((2, 64, 128), f32),
        vmem((4, 2, 64, 128), f32),
        vmem((8, 4, 8, 256), f32),
        vmem((4, 8, 8, 128), f32),
        vmem((4, 4, 8, 256), f32),
        vmem((10, 8, 128), f32),
        vmem((10, 8, 8, 128), f32),
        vmem((4, 8, 128), f32),
        vmem((2, 8, 128), f32),
        vmem((2, 8, 8, 128), f32),
        vmem((4, 8, 128), f32),
        vmem((4, 8, 256), f32),
        vmem((8, 128), f32),
        vmem((4, 128, 128), f32),
        vmem((6, 128, 128), f32),
        vmem((128, 128), f32),
        vmem((leaves, members, part), f32),
        vmem((leaves, members, 128), f32),
        vmem((4, leaves, members, 128), f32),
        vmem((members, 384), f32),
        vmem((8, members, 384), f32),
        vmem((members, 256), f32),
        vmem((4, members, 256), f32),
        vmem((members, 128), f32),
        vmem((4, members, 128), f32),
        pltpu.SemaphoreType.DMA((24,)),
        pltpu.SemaphoreType.DMA((COPIES,)),
        pltpu.SemaphoreType.DMA((COPIES,)),
        pltpu.SemaphoreType.DMA((11,)),
        pltpu.SemaphoreType.DMA((9,)),
    ]
    result = pl.pallas_call(
        kernel,
        out_shape=jax.ShapeDtypeStruct((leaves, members, part), f32),
        in_specs=[pl.BlockSpec(memory_space=pl.ANY)] * 6,
        out_specs=pl.BlockSpec(memory_space=pltpu.VMEM),
        scratch_shapes=scratch,
        compiler_params=pltpu.CompilerParams(
            collective_id=0, has_side_effects=True, vmem_limit_bytes=48 * 2**20
        ),
    )(*inputs)
    return jnp.transpose(result, (1, 0, 2))


def solution(mesh):
    in_specs = (
        P(None, "leaf", "sub"),
        P("leaf", None),
        P("leaf", "sub", None),
        P(None, None, "leaf", "sub"),
        P(None, None, "leaf", "sub"),
        P("leaf", None, None),
    )
    return jax.shard_map(
        per_device, mesh=mesh, in_specs=in_specs, out_specs=P(None, "leaf", "sub"), check_vma=False
    )
```

time: 567 us -> 45.4 us (0.08)
  waiting for transfers between devices: 292 us -> 0 us
  blocking collectives: 221 us -> 0 us
  Pallas kernels: 0 us -> 38.9 us
  matrix products: 26.1 us -> 0 us
  between operations: 15.3 us -> 0.01 us
    psum x2 -> x0, waiting for transfers between devices: 292 us -> none  [per_device(): lax.psum(selector[:, None, None] * positioned_rows[None], ('leaf', 'sub'))]
    psum x5 -> x0, blocking collectives: 208 us -> none  [the longest x3 190 us: per_device(): lax.psum(selector[:, None, None] * positioned_rows[None], ('leaf', 'sub'))]
    pallas_call x0 -> x1, Pallas kernels: none -> 38.9 us  [per_device(): pl.pallas_call(kernel, out_shape=jax.ShapeDtypeStruct((leaves, members, p...]
    dot_general x23 -> x0, matrix products: 26.1 us -> none  [the longest x1 8.8 us: per_device(): jnp.einsum('ljk,mlk->mlj', selection, gathered, precision=exact_precision)]
    all_gather x1 -> x0, blocking collectives: 12.3 us -> none  [per_device(): gathered = lax.all_gather(right_sides, 'sub', axis=2, tiled=True)]
  transfers between devices with their start and end apart: 3 -> 0, of which waited for: 2 -> 0; matrix products, arithmetic and copies ran while one was open for 0% -> 0% of each run, Pallas kernels for 0% -> 0%
where the time goes in v1:
time: 45.4 us; the launch traced here: 45.1 us
  Pallas kernels  38.9 us (86%)
  local copies, waits for them, and re-layouts  6.18 us (14%)
    pallas_call x1, Pallas kernels, per_device(): pl.pallas_call(kernel, out_shape=jax.ShapeDtypeStruct((leaves, members, p...  38.9 us
    unnamed x10, local copies, waits for them, and re-layouts  5.5 us

profile of v1, /device:TPU:1, one launch (start us, length us, event | category | flops | bytes accessed | tf_op | source)
XLA Modules:
  0.0 45.1 jit_solution(4139686486463496929)
XLA Ops:
  0.0 0.0 copy-start
  0.0 1.5 %copy-done = f32[7,64,4,256]{3,2,1,0:T(4,128)S(1)} copy-done((f32[7,64,4,256]{3,2,1,0:T(4,128)S(1)}, f32[7,64,4,256]{3,2,1,0:T(4,128)}, u32[]{:S(2)}) %copy-start) | copy-done | bytes 1835032
  1.5 0.0 copy-start.1
  1.5 1.5 %copy-done.1 = f32[7,64,4,256]{3,2,1,0:T(4,128)S(1)} copy-done((f32[7,64,4,256]{3,2,1,0:T(4,128)S(1)}, f32[7,64,4,256]{3,2,1,0:T(4,128)}, u32[]{:S(2)}) %copy-start.1) | copy-done | bytes 1835032
  3.0 0.0 copy-start.2
  3.0 0.9 %copy-done.2 = f32[4,128,128]{2,1,0:T(8,128)S(1)} copy-done((f32[4,128,128]{2,1,0:T(8,128)S(1)}, f32[4,128,128]{2,1,0:T(8,128)}, u32[]{:S(2)}) %copy-start.2) | copy-done | bytes 262168
  4.0 0.0 copy-start.3
  4.0 0.8 %copy-done.3 = f32[16,4,256]{2,1,0:T(4,128)S(1)} copy-done((f32[16,4,256]{2,1,0:T(4,128)S(1)}, f32[16,4,256]{2,1,0:T(4,128)}, u32[]{:S(2)}) %copy-start.3) | copy-done | bytes 65560
  4.8 0.0 copy-start.4
  4.8 0.7 %copy-done.4 = s32[4,1024]{1,0:T(4,128)S(1)} copy-done((s32[4,1024]{1,0:T(4,128)S(1)}, s32[4,1024]{1,0:T(4,128)}, u32[]{:S(2)}) %copy-start.4) | copy-done | bytes 16408
  5.5 38.9 %shard_map.64 = f32[4,16,256]{2,1,0:T(8,128)S(1)} custom-call(f32[16,4,256]{2,1,0:T(4,128)S(1)} %copy-done.3, s32[4,1024]{1,0:T(4,128)S(1)} %copy-done.4, f32[4,256,1024]{2,1,0:T(8,128)} %inverse.1, f32[7,64,4,256]{3,2,1,0:T(4,128)S(1)} %copy-done, f32[7,64,4,256]{3,2,1,0:T(4,128)S(1)} %copy-done.1, f32[4,128,128]{2,1,0:T(8,128)S(1)} %copy-done.2), custom_call_target="tpu_custom_call" | custom-call | tf_op jit(solution)/shard_map/pallas_call | solution.py:420
  44.5 0.7 %copy.7 = f32[16,4,256]{2,1,0:T(4,128)} copy(f32[16,4,256]{2,0,1:T(8,128)S(1)} %bitcast.1) | data formatting | bytes 131072 | tf_op jit(solution)/shard_map/transpose | solution.py:430
Async XLA Ops:
  0.0 1.5 %copy-start = (f32[7,64,4,256]{3,2,1,0:T(4,128)S(1)}, f32[7,64,4,256]{3,2,1,0:T(4,128)}, u32[]{:S(2)}) copy-start(f32[7,64,4,256]{3,2,1,0:T(4,128)} %left.1) | copy-start | bytes 5505028
  1.5 1.5 %copy-start.1 = (f32[7,64,4,256]{3,2,1,0:T(4,128)S(1)}, f32[7,64,4,256]{3,2,1,0:T(4,128)}, u32[]{:S(2)}) copy-start(f32[7,64,4,256]{3,2,1,0:T(4,128)} %column.1) | copy-start | bytes 5505028
  3.0 0.9 %copy-start.2 = (f32[4,128,128]{2,1,0:T(8,128)S(1)}, f32[4,128,128]{2,1,0:T(8,128)}, u32[]{:S(2)}) copy-start(f32[4,128,128]{2,1,0:T(8,128)} %cores.1) | copy-start | bytes 786436
  4.0 0.8 %copy-start.3 = (f32[16,4,256]{2,1,0:T(4,128)S(1)}, f32[16,4,256]{2,1,0:T(4,128)}, u32[]{:S(2)}) copy-start(f32[16,4,256]{2,1,0:T(4,128)} %right.1) | copy-start | bytes 196612
  4.8 0.7 %copy-start.4 = (s32[4,1024]{1,0:T(4,128)S(1)}, s32[4,1024]{1,0:T(4,128)}, u32[]{:S(2)}) copy-start(s32[4,1024]{1,0:T(4,128)} %order.1) | copy-start | bytes 49156

commit v2 on v1

--- a/solution.py
+++ b/solution.py
@@ -424,7 +424,7 @@
         out_specs=pl.BlockSpec(memory_space=pltpu.VMEM),
         scratch_shapes=scratch,
         compiler_params=pltpu.CompilerParams(
-            collective_id=0, has_side_effects=True, vmem_limit_bytes=48 * 2**20
+            collective_id=0, has_side_effects=True, vmem_limit_bytes=63 * 2**20
         ),
     )(*inputs)
     return jnp.transpose(result, (1, 0, 2))

time: 45.4 us -> 39.2 us (0.86)
  local copies, waits for them, and re-layouts: 6.18 us -> 1.51 us
  Pallas kernels: 38.9 us -> 37.6 us
    unnamed x10 -> x0, local copies, waits for them, and re-layouts: 5.5 us -> none
    pallas_call x1, Pallas kernels: 38.9 us -> 37.6 us  [per_device(): pl.pallas_call(kernel, out_shape=jax.ShapeDtypeStruct((leaves, members, p...]
    transpose x1, local copies, waits for them, and re-layouts: 0.67 us -> 1.51 us  [per_device(): return jnp.transpose(result, (1, 0, 2))]
where the time goes in v2:
time: 39.2 us; the launch traced here: 39.1 us
  Pallas kernels  37.6 us (96%)
  local copies, waits for them, and re-layouts  1.51 us (4%)
    pallas_call x1, Pallas kernels, per_device(): pl.pallas_call(kernel, out_shape=jax.ShapeDtypeStruct((leaves, members, p...  37.6 us
    transpose x1, local copies, waits for them, and re-layouts, per_device(): return jnp.transpose(result, (1, 0, 2))  1.51 us

profile of v2, /device:TPU:1, one launch (start us, length us, event | category | flops | bytes accessed | tf_op | source)
XLA Modules:
  0.0 39.1 jit_solution(3458519609179709988)
XLA Ops:
  0.0 37.6 %shard_map.64 = f32[4,16,256]{2,1,0:T(8,128)} custom-call(f32[16,4,256]{2,1,0:T(4,128)} %right.1, s32[4,1024]{1,0:T(4,128)} %order.1, f32[4,256,1024]{2,1,0:T(8,128)} %inverse.1, f32[7,64,4,256]{3,2,1,0:T(4,128)} %left.1, f32[7,64,4,256]{3,2,1,0:T(4,128)} %column.1, f32[4,128,128]{2,1,0:T(8,128)} %cores.1), custom_call_target="tpu_custom_call" | custom-call | tf_op jit(solution)/shard_map/pallas_call | solution.py:420
  37.6 1.5 %copy.7 = f32[16,4,256]{2,1,0:T(4,128)} copy(f32[16,4,256]{2,0,1:T(8,128)} %bitcast.1) | data formatting | bytes 131072 | tf_op jit(solution)/shard_map/transpose | solution.py:430

commit v3 on v2

--- a/solution.py
+++ b/solution.py
@@ -11,7 +11,7 @@
 f32, bf16 = jnp.float32, jnp.bfloat16
 
 SLOT_LEVELS = (4, 5, 6, 7, 3, 2, 1)
-COPIES = 96
+STEPS = 16
 
 
 def split(value):
@@ -63,46 +63,44 @@
     y_peers = [(8 * x + 2 * lax.rem(y + d, 4) + c, z) for d in (1, 2, 3)]
     x_peers = [(8 * lax.rem(x + d, 4) + 2 * y + c, z) for d in (1, 2, 3)]
 
-    count = [0]
-    started = []
-
-    def send(src, dst, device):
-        i = count[0]
-        count[0] += 1
-        copy = pltpu.make_async_remote_copy(
-            src_ref=src, dst_ref=dst, send_sem=send_sem.at[i], recv_sem=recv_sem.at[i],
+    steps = []
+
+    def send(parts, landed):
+        i = len(steps)
+        for src, dst, device in parts:
+            remote(send_sem.at[i], recv_sem.at[i], src, dst, device).start()
+        steps.append(remote(send_sem.at[i], recv_sem.at[i], landed, landed, sibling))
+        return steps[i]
+
+    def remote(sent, received, src, dst, device):
+        return pltpu.make_async_remote_copy(
+            src_ref=src, dst_ref=dst, send_sem=sent, recv_sem=received,
             device_id=device, device_id_type=MESH,
         )
-        copy.start()
-        started.append(copy)
-        return copy
-
-    def receive(copies):
-        for copy in copies:
-            copy.wait_recv()
 
     loads = []
 
-    def load(src, dst):
-        copy = pltpu.make_async_copy(src, dst, load_sem.at[len(loads)])
-        copy.start()
-        loads.append(copy)
-        return copy
-
-    rhs_loads = [load(right.at[:, l, :], rhs.at[z, l]) for l in range(leaves)]
-    order_load = load(order, index)
-    basis_loads = [load(column.at[:, :, l, :], v32.at[l]) for l in range(leaves)]
-    basis_loads += [load(left.at[:, :, l, :], u32.at[l]) for l in range(leaves)]
-    core_load = load(cores, core)
-    inverse_loads = [load(inverse.at[l], inv.at[l]) for l in range(leaves)]
+    def load(parts, landed):
+        i = len(loads)
+        for src, dst in parts:
+            pltpu.make_async_copy(src, dst, load_sem.at[i]).start()
+        loads.append(pltpu.make_async_copy(landed, landed, load_sem.at[i]))
+        return loads[i]
+
+    rhs_load = load([(right.at[:, l, :], rhs.at[z, l]) for l in range(leaves)], rhs.at[z])
+    order_load = load([(order, index)], index)
+    column_load = load([(column.at[:, :, l, :], v32.at[l]) for l in range(leaves)], v32)
+    left_load = load([(left.at[:, :, l, :], u32.at[l]) for l in range(leaves)], u32)
+    core_load = load([(cores, core)], core)
+    inverse_load = load([(inverse, inv)], inv)
 
     barrier = pltpu.get_barrier_semaphore()
     peers = zc_peers + y_peers + x_peers
     for peer in peers:
         pl.semaphore_signal(barrier, inc=1, device_id=peer, device_id_type=MESH)
 
-    for copy in basis_loads:
-        copy.wait()
+    column_load.wait()
+    left_load.wait()
     for l in range(leaves):
         for slot, level in enumerate(SLOT_LEVELS):
             norm = 1.0 / math.sqrt(1024 * 2 ** (level - 1))
@@ -133,25 +131,29 @@
     for n in range(2):
         g21p[n] = low_low(q1[320:384, 256 * n : 256 * n + 128], q1[320:384, 256 * n + 128 : 256 * n + 256])
 
-    for copy in rhs_loads:
-        copy.wait()
+    rhs_load.wait()
     core_load.wait()
     pl.semaphore_wait(barrier, len(peers))
-    rhs_copies = [[send(rhs.at[z, l], rhs.at[z, l], peer) for peer in z_peers] for l in range(leaves)]
+    three = pl.ds(0, 3)
+    seven = pl.ds(0, 7)
+    rhs_steps = [
+        send([(rhs.at[z, l], rhs.at[z, l], peer) for peer in z_peers], rhs.at[three, l])
+        for l in range(leaves)
+    ]
 
     last_column = lax.rem(leaf, 8) == 7
 
-    def c_copy(i, j, src, dst, device):
-        return pltpu.make_async_remote_copy(
-            src_ref=src, dst_ref=dst, send_sem=c_send.at[i], recv_sem=c_recv.at[j],
-            device_id=device, device_id_type=MESH,
-        )
-
-    along_x = [c_copy(d, d, core.at[3], xc.at[x], x_peers[d]) for d in range(3)]
-    along_y_one = [c_copy(3 + d, 3 + y, core.at[3], cb.at[y], y_peers[d]) for d in range(3)]
-    along_y_three = [c_copy(6 + d, 6, xc.at[pl.ds(0, 3)], cb.at[pl.ds(3, 3)], y_peers[d]) for d in range(3)]
-    to_sibling = c_copy(9, 7, cb, cb, sibling)
-    third = c_copy(10, 8, core.at[3], c3, sibling)
+    def core_copies(i, parts):
+        return [remote(c_send.at[i], c_recv.at[i], *each) for each in parts]
+
+    along_x = core_copies(0, [(core.at[3], xc.at[x], peer) for peer in x_peers])
+    along_y_one = core_copies(1, [(core.at[3], cb.at[y], peer) for peer in y_peers])
+    along_y_three = core_copies(1, [(xc.at[three], cb.at[pl.ds(3, 3)], peer) for peer in y_peers])
+    to_sibling = remote(c_send.at[2], c_recv.at[2], cb, cb, sibling)
+    third = remote(c_send.at[3], c_recv.at[3], core.at[3], c3, sibling)
+
+    def core_wait(i, landed):
+        return remote(c_send.at[i], c_recv.at[i], landed, landed, sibling)
 
     @pl.when(last_column)
     def _():
@@ -172,14 +174,16 @@
     rs[me] = q3[:, me]
     g21[z] = g21p[...]
     order_load.wait()
-    for copy in inverse_loads:
-        copy.wait()
-    g21_copies = [send(g21p, g21.at[z], peer) for peer in z_peers]
-    rs_copies = [send(q3.at[:, i], rs.at[me], peer) for i, peer in zip(zc_index, zc_peers, strict=True)]
-
-    r1_copies = []
-    for l in range(leaves):
-        receive(rhs_copies[l])
+    inverse_load.wait()
+    g21_step = send([(g21p, g21.at[z], peer) for peer in z_peers], g21.at[three])
+    rs_step = send(
+        [(q3.at[:, i], rs.at[me], peer) for i, peer in zip(zc_index, zc_peers, strict=True)],
+        rs.at[seven],
+    )
+
+    r1_steps = []
+    for l in range(leaves):
+        rhs_steps[l].wait_recv()
         pieces = []
         for u in range(8):
             place = index[l : l + 1, 128 * u : 128 * u + 128]
@@ -196,7 +200,8 @@
         r1p[l] = product(nt, values, vh[l, 5:7].reshape(128, part), vl[l, 5:7].reshape(128, part))
         if l % 2 == 1:
             pair = pl.ds(l - 1, 2)
-            r1_copies += [send(r1p.at[pair], r1.at[z, pair], peer) for peer in z_peers]
+            parts = [(r1p.at[pair], r1.at[z, pair], peer) for peer in z_peers]
+            r1_steps.append(send(parts, r1.at[three, pair]))
     r1[z] = r1p[...]
 
     raw = None
@@ -206,8 +211,7 @@
 
     @pl.when(last_column)
     def _():
-        for copy in along_x:
-            copy.wait_recv()
+        core_wait(0, xc.at[three]).wait_recv()
         for copy in along_y_three:
             copy.start()
         cb[3:6] = xc[0:3]
@@ -220,23 +224,24 @@
                 copy.start()
             cb[y] = core[3]
 
-    receive(rs_copies)
+    rs_step.wait_recv()
     sum_a = rs[0] + rs[2] + rs[4] + rs[6]
     sum_b = rs[1] + rs[3] + rs[5] + rs[7]
     g3p[...] = low_low(sum_a[:, :, :128], sum_b[:, :, :128])
     g3[:, me] = g3p[...]
     ysp[...] = sum_a + sum_b
     ys[y] = ysp[...]
-    g3_copies = [send(g3p, g3.at[:, me], peer) for peer in zc_peers]
-    ys_copies = [send(ysp, ys.at[y], peer) for peer in y_peers]
-    receive(g21_copies)
+    g3_step = send([(g3p, g3.at[:, me], peer) for peer in zc_peers], g3.at[:, seven])
+    ys_step = send([(ysp, ys.at[y], peer) for peer in y_peers], ys.at[three])
+    g21_step.wait_recv()
     coupling = g21[0] + g21[1] + g21[2] + g21[3]
     zeros = jnp.zeros((64, 128), f32)
     coupling = jnp.concatenate(
         [jnp.concatenate([coupling[0], zeros], 1), jnp.concatenate([zeros, coupling[1]], 1)], 0
     )
 
-    receive(r1_copies)
+    for step in r1_steps:
+        step.wait_recv()
     s = [r1[0, l] + r1[1, l] + r1[2, l] + r1[3, l] for l in range(leaves)]
     s1 = [apply_rows(high_high(s[2 * n], s[2 * n + 1]), core[2 * n]) for n in range(2)]
     p2 = low_low(s[0] + s[1], s[2] + s[3]) - apply_rows(jnp.concatenate(s1, 1), coupling)
@@ -248,7 +253,7 @@
         high_high(s1[1], s2),
     ]
     r2p[...] = raw - product(nt, jnp.concatenate(own, 1), q1h[...], q1l[...])
-    r2_copies = [send(r2p, r2.at[me], peer) for peer in zc_peers]
+    r2_step = send([(r2p, r2.at[me], peer) for peer in zc_peers], r2.at[seven])
     r2[me] = r2p[...]
 
     def correct(l, coefficients, levels):
@@ -260,18 +265,17 @@
 
     @pl.when(c == 1)
     def _():
-        for j in range(3):
-            @pl.when(y != j)
-            def _():
-                c_copy(3, 3 + j, core.at[3], cb.at[j], sibling).wait_recv()
-
-        @pl.when(y != 3)
+        @pl.when(y == 3)
         def _():
-            along_y_three[0].wait_recv()
+            core_wait(1, cb.at[three]).wait_recv()
+
+        @pl.when(y < 3)
+        def _():
+            core_wait(1, cb.at[pl.ds(0, 5)]).wait_recv()
 
         to_sibling.start()
 
-    receive(ys_copies)
+    ys_step.wait_recv()
     for n in range(2):
         g45p[4 * n : 4 * n + 4] = high_high(ys[2 * n, :, :, :128], ys[2 * n + 1, :, :, :128])
     halves = [ys[0, 2:4, :, 128:] + ys[1, 2:4, :, 128:], ys[2, 2:4, :, 128:] + ys[3, 2:4, :, 128:]]
@@ -279,35 +283,35 @@
     xsp[...] = halves[0][1] + halves[1][1]
     g45[:, me] = g45p[...]
     xs[x] = xsp[...]
-    xs_copies = [send(xsp, xs.at[x], peer) for peer in x_peers]
-    g45_copies = [send(g45p, g45.at[:, me], peer) for peer in zc_peers]
-
-    receive(g3_copies)
+    xs_step = send([(xsp, xs.at[x], peer) for peer in x_peers], xs.at[three])
+    g45_step = send([(g45p, g45.at[:, me], peer) for peer in zc_peers], g45.at[:, seven])
+
+    g3_step.wait_recv()
 
     @pl.when(c == 1)
     def _():
         third.wait_recv()
 
-    receive(r2_copies)
+    r2_step.wait_recv()
     p_a = r2[0] + r2[2] + r2[4] + r2[6]
     p_b = r2[1] + r2[3] + r2[5] + r2[7]
     s3 = apply_rows(low_low(p_a[:, 256:], p_b[:, 256:]), c3[...])
     r3p[...] = p_a[:, :256] + p_b[:, :256] - apply_rows(s3, g3[...].reshape(256, 128))
-    r3_copies = [send(r3p, r3.at[y], peer) for peer in y_peers]
+    r3_step = send([(r3p, r3.at[y], peer) for peer in y_peers], r3.at[three])
     r3[y] = r3p[...]
 
-    receive(xs_copies)
+    xs_step.wait_recv()
     for n in range(2):
         g6p[n] = high_high(xs[2 * n], xs[2 * n + 1])
     g6[:, me] = g6p[...]
-    g6_copies = [send(g6p, g6.at[:, me], peer) for peer in zc_peers]
+    g6_step = send([(g6p, g6.at[:, me], peer) for peer in zc_peers], g6.at[:, seven])
 
     @pl.when(c == 0)
     def _():
         to_sibling.wait_recv()
 
-    receive(g45_copies)
-    receive(r3_copies)
+    g45_step.wait_recv()
+    r3_step.wait_recv()
     s4, below = [], []
     for n in range(2):
         p4 = low_low(r3[2 * n, :, :128], r3[2 * n + 1, :, :128])
@@ -315,7 +319,7 @@
         below.append(r3[2 * n] + r3[2 * n + 1] - apply_rows(s4[n], g45[4 * n : 4 * n + 4].reshape(256, 128)))
     s5 = apply_rows(high_high(below[0][:, :128], below[1][:, :128]), cb[1])
     r4p[...] = below[0][:, 128:] + below[1][:, 128:] - apply_rows(s5, g45[8:10].reshape(128, 128))
-    r4_copies = [send(r4p, r4.at[x], peer) for peer in x_peers]
+    r4_step = send([(r4p, r4.at[x], peer) for peer in x_peers], r4.at[three])
     r4[x] = r4p[...]
 
     own3 = jnp.where(c == 0, s3, turn(s3))
@@ -326,7 +330,7 @@
     for l in range(leaves):
         field[l] = field[l] - correct(l, own34, (2, 4)) - correct(l, own5[:, :64], (4, 5))
 
-    receive(g6_copies)
+    g6_step.wait_recv()
     coupling = jnp.concatenate(
         [
             jnp.concatenate([g6[0].reshape(64, 128), zeros], 1),
@@ -334,7 +338,7 @@
         ],
         0,
     )
-    receive(r4_copies)
+    r4_step.wait_recv()
     s6 = [apply_rows(low_low(r4[2 * n], r4[2 * n + 1]), cb[3 + 2 * n]) for n in range(2)]
     p7 = high_high(r4[0] + r4[1], r4[2] + r4[3]) - apply_rows(jnp.concatenate(s6, 1), coupling)
     s7 = apply_rows(p7, cb[4])
@@ -345,13 +349,13 @@
     for l in range(leaves):
         out[l] = field[l] - correct(l, own67, (5, 7))
 
-    for copy in started:
-        copy.wait_send()
+    for step in steps:
+        step.wait_send()
 
     @pl.when(last_column)
     def _():
-        for copy in along_x + along_y_three:
-            copy.wait_send()
+        core_wait(0, xc.at[three]).wait_send()
+        core_wait(1, inv.at[0, pl.ds(0, 144)]).wait_send()
 
     @pl.when(c == 1)
     def _():
@@ -359,8 +363,7 @@
 
         @pl.when(y < 3)
         def _():
-            for copy in along_y_one:
-                copy.wait_send()
+            core_wait(1, cb.at[three]).wait_send()
 
     @pl.when(c == 0)
     def _():
@@ -411,11 +414,11 @@
         vmem((4, members, 256), f32),
         vmem((members, 128), f32),
         vmem((4, members, 128), f32),
-        pltpu.SemaphoreType.DMA((24,)),
-        pltpu.SemaphoreType.DMA((COPIES,)),
-        pltpu.SemaphoreType.DMA((COPIES,)),
-        pltpu.SemaphoreType.DMA((11,)),
-        pltpu.SemaphoreType.DMA((9,)),
+        pltpu.SemaphoreType.DMA((6,)),
+        pltpu.SemaphoreType.DMA((STEPS,)),
+        pltpu.SemaphoreType.DMA((STEPS,)),
+        pltpu.SemaphoreType.DMA((4,)),
+        pltpu.SemaphoreType.DMA((4,)),
     ]
     result = pl.pallas_call(
         kernel,
@@ -424,7 +427,7 @@
         out_specs=pl.BlockSpec(memory_space=pltpu.VMEM),
         scratch_shapes=scratch,
         compiler_params=pltpu.CompilerParams(
-            collective_id=0, has_side_effects=True, vmem_limit_bytes=63 * 2**20
+            collective_id=0, has_side_effects=True, vmem_limit_bytes=53 * 2**20 + 832 * 2**10
         ),
     )(*inputs)
     return jnp.transpose(result, (1, 0, 2))

time: 39.2 us -> 36.7 us (0.936)
  Pallas kernels: 37.6 us -> 35.1 us
    pallas_call x1, Pallas kernels: 37.6 us -> 35.1 us  [per_device(): pl.pallas_call(kernel, out_shape=jax.ShapeDtypeStruct((leaves, members, p...]
    transpose x1, local copies, waits for them, and re-layouts: 1.51 us -> 0.67 us  [per_device(): return jnp.transpose(result, (1, 0, 2))]
    unnamed x0 -> x2, local copies, waits for them, and re-layouts: none -> 0.72 us
where the time goes in v3:
time: 36.7 us; the launch traced here: 36.5 us
  Pallas kernels  35.1 us (96%)
  local copies, waits for them, and re-layouts  1.39 us (4%)
    pallas_call x1, Pallas kernels, per_device(): pl.pallas_call(kernel, out_shape=jax.ShapeDtypeStruct((leaves, members, p...  35.1 us

profile of v3, /device:TPU:1, one launch (start us, length us, event | category | flops | bytes accessed | tf_op | source)
XLA Modules:
  0.0 36.5 jit_solution(897940654808063771)
XLA Ops:
  0.0 0.0 copy-start
  0.0 0.7 %copy-done = s32[4,1024]{1,0:T(4,128)S(1)} copy-done((s32[4,1024]{1,0:T(4,128)S(1)}, s32[4,1024]{1,0:T(4,128)}, u32[]{:S(2)}) %copy-start) | copy-done | bytes 16408
  0.7 35.1 %shard_map.64 = f32[4,16,256]{2,1,0:T(8,128)S(1)} custom-call(f32[16,4,256]{2,1,0:T(4,128)} %right.1, s32[4,1024]{1,0:T(4,128)S(1)} %copy-done, f32[4,256,1024]{2,1,0:T(8,128)} %inverse.1, f32[7,64,4,256]{3,2,1,0:T(4,128)} %left.1, f32[7,64,4,256]{3,2,1,0:T(4,128)} %column.1, f32[4,128,128]{2,1,0:T(8,128)} %cores.1), custom_call_target="tpu_custom_call" | custom-call | tf_op jit(solution)/shard_map/pallas_call | solution.py:423
  35.8 0.7 %copy.7 = f32[16,4,256]{2,1,0:T(4,128)} copy(f32[16,4,256]{2,0,1:T(8,128)S(1)} %bitcast.1) | data formatting | bytes 131072 | tf_op jit(solution)/shard_map/transpose | solution.py:433
Async XLA Ops:
  0.0 0.7 %copy-start = (s32[4,1024]{1,0:T(4,128)S(1)}, s32[4,1024]{1,0:T(4,128)}, u32[]{:S(2)}) copy-start(s32[4,1024]{1,0:T(4,128)} %order.1) | copy-start | bytes 49156

commit v4 on v3

--- a/solution.py
+++ b/solution.py
@@ -10,8 +10,7 @@
 MESH = pl.DeviceIdType.MESH
 f32, bf16 = jnp.float32, jnp.bfloat16
 
-SLOT_LEVELS = (4, 5, 6, 7, 3, 2, 1)
-STEPS = 16
+STEPS = 19
 
 
 def split(value):
@@ -43,12 +42,13 @@
     out,
     rhs, index, inv, u32, v32, core,
     uh, ul, vh, vl,
-    q1, q1h, q1l, q3, g21p, g21, rs, g3, ys, g45p, g45, xs, g6p, g6, g3p, ysp, xsp,
+    fold_h, fold_l, low, q3a, q3b, g21p, g21, rsa, rsb, g3, ys, g45p, g45, xs, g6p, g6, g3p, ysp, xsp,
     xc, cb, c3,
-    field, r1p, r1, r2p, r2, r3p, r3, r4p, r4,
+    field, coefficients, r1p, r1, r2p, r2, r3p, r3, r4p, r4,
     load_sem, send_sem, recv_sem, c_send, c_recv,
 ):
     members, leaves, part = right.shape
+    size = order.shape[1]
     leaf, z = lax.axis_index("leaf"), lax.axis_index("sub")
     c = lax.rem(leaf, 2)
     y = lax.rem(lax.div(leaf, 2), 4)
@@ -88,10 +88,13 @@
         return loads[i]
 
     rhs_load = load([(right.at[:, l, :], rhs.at[z, l]) for l in range(leaves)], rhs.at[z])
-    order_load = load([(order, index)], index)
-    column_load = load([(column.at[:, :, l, :], v32.at[l]) for l in range(leaves)], v32)
+    order_load = load([(order.at[pl.ds(l, 1)], index.at[l]) for l in range(leaves)], index)
+    core_load = load([(cores, core)], core)
+    slots = [(slice(3, 7), slice(0, 4)), (2, 4), (1, 5), (0, 6)]
+    column_load = load(
+        [(column.at[a, :, l, :], v32.at[l, b]) for l in range(leaves) for a, b in slots], v32
+    )
     left_load = load([(left.at[:, :, l, :], u32.at[l]) for l in range(leaves)], u32)
-    core_load = load([(cores, core)], core)
     inverse_load = load([(inverse, inv)], inv)
 
     barrier = pltpu.get_barrier_semaphore()
@@ -99,40 +102,7 @@
     for peer in peers:
         pl.semaphore_signal(barrier, inc=1, device_id=peer, device_id_type=MESH)
 
-    column_load.wait()
-    left_load.wait()
-    for l in range(leaves):
-        for slot, level in enumerate(SLOT_LEVELS):
-            norm = 1.0 / math.sqrt(1024 * 2 ** (level - 1))
-            vh[l, slot], vl[l, slot] = split(v32[l, level - 1] * norm)
-        for k in range(7):
-            uh[l, k], ul[l, k] = split(u32[l, k])
-
-    def gram(l, slots, levels):
-        a_high, a_low = (t[l, slots[0]:slots[1]].reshape(-1, part) for t in (vh, vl))
-        b_high, b_low = (t[l, levels[0]:levels[1]].reshape(-1, part) for t in (uh, ul))
-        return nt(a_high, b_high) + nt(a_low, b_high) + nt(a_high, b_low)
-
-    low_lanes = lax.broadcasted_iota(jnp.int32, (1, 128), 1) < 64
-
-    def turn(a):
-        return pltpu.roll(a, 64, a.ndim - 1)
-
-    def low_low(a, b):
-        return jnp.where(low_lanes, a, turn(b))
-
-    def high_high(a, b):
-        return jnp.where(low_lanes, turn(a), b)
-
-    for l in range(leaves):
-        block = gram(l, (0, 6), (0, 2))
-        q1[:, 128 * l : 128 * l + 128] = block
-        q1h[:, 128 * l : 128 * l + 128], q1l[:, 128 * l : 128 * l + 128] = split(block)
-    for n in range(2):
-        g21p[n] = low_low(q1[320:384, 256 * n : 256 * n + 128], q1[320:384, 256 * n + 128 : 256 * n + 256])
-
     rhs_load.wait()
-    core_load.wait()
     pl.semaphore_wait(barrier, len(peers))
     three = pl.ds(0, 3)
     seven = pl.ds(0, 7)
@@ -155,6 +125,8 @@
     def core_wait(i, landed):
         return remote(c_send.at[i], c_recv.at[i], landed, landed, sibling)
 
+    core_load.wait()
+
     @pl.when(last_column)
     def _():
         for copy in along_x:
@@ -166,27 +138,65 @@
         third.start()
         c3[...] = core[3]
 
-    total = None
-    for l in range(leaves):
-        block = gram(l, (0, 4), (2, 6))
-        total = block if total is None else total + block
-    q3[...] = total.reshape(4, 8, 8, 256)
-    rs[me] = q3[:, me]
+    low_lanes = lax.broadcasted_iota(jnp.int32, (1, 128), 1) < 64
+
+    def norm(level):
+        return 1.0 / math.sqrt(size * 2 ** (level - 1))
+
+    def turn(a):
+        return pltpu.roll(a, 64, a.ndim - 1)
+
+    def low_low(a, b):
+        return jnp.where(low_lanes, a, turn(b))
+
+    def high_high(a, b):
+        return jnp.where(low_lanes, turn(a), b)
+
+    def each_leaf(body, unroll=False):
+        lax.fori_loop(0, leaves, lambda l, none: body(l), None, unroll=unroll)
+
+    def gram(l, slots, levels):
+        a_high, a_low = split(v32[l, slots[0]:slots[1]].reshape(-1, part))
+        b_high, b_low = split(u32[l, levels[0]:levels[1]].reshape(-1, part))
+        return nt(a_high, b_high) + nt(a_low, b_high) + nt(a_high, b_low)
+
+    column_load.wait()
+    left_load.wait()
+    for n in range(2):
+        g21p[n] = low_low(*(gram(2 * n + j, (5, 6), (0, 2)) for j in range(2)))
     g21[z] = g21p[...]
+    g21_step = send([(g21p, g21.at[z], peer) for peer in z_peers], g21.at[three])
+
+    total = gram(0, (0, 4), (2, 6))
+    for l in range(1, leaves):
+        total += gram(l, (0, 4), (2, 6))
+    q3a[...] = total[:128, :128].reshape(2, 8, 8, 128)
+    q3b[...] = total[128:].reshape(2, 8, 8, 256)
+    rsa[me] = q3a[:, me]
+    rsb[me] = q3b[:, me]
+    zc_pairs = list(zip(zc_index, zc_peers, strict=True))
+    rsa_step = send([(q3a.at[:, i], rsa.at[me], peer) for i, peer in zc_pairs], rsa.at[seven])
+    rsb_step = send([(q3b.at[:, i], rsb.at[me], peer) for i, peer in zc_pairs], rsb.at[seven])
+
+    def split_bases(l):
+        for k in range(7):
+            vh[l, k], vl[l, k] = split(v32[l, k])
+            uh[l, k], ul[l, k] = split(u32[l, k])
+
+    each_leaf(split_bases, True)
     order_load.wait()
     inverse_load.wait()
-    g21_step = send([(g21p, g21.at[z], peer) for peer in z_peers], g21.at[three])
-    rs_step = send(
-        [(q3.at[:, i], rs.at[me], peer) for i, peer in zip(zc_index, zc_peers, strict=True)],
-        rs.at[seven],
-    )
-
-    r1_steps = []
+
+    first = len(steps)
     for l in range(leaves):
-        rhs_steps[l].wait_recv()
+        steps.append(remote(send_sem.at[first + l], recv_sem.at[first + l], r1.at[three, l], r1.at[three, l], sibling))
+    r1_steps = steps[first:]
+
+    def solve_leaf(l):
+        remote(send_sem.at[l], recv_sem.at[l], rhs.at[three, l], rhs.at[three, l], sibling).wait_recv()
         pieces = []
         for u in range(8):
-            place = index[l : l + 1, 128 * u : 128 * u + 128]
+            place = index[l, :, 128 * u : 128 * u + 128]
             lane = jnp.broadcast_to(place & 127, (members, 128))
             tile = jnp.broadcast_to(place >> 7, (members, 128))
             piece = jnp.zeros((members, 128), f32)
@@ -194,20 +204,25 @@
                 source = rhs[t // 2, l, :, 128 * (t % 2) : 128 * (t % 2) + 128]
                 piece = jnp.where(tile == t, jnp.take_along_axis(source, lane, axis=1), piece)
             pieces.append(piece)
-        ordered = jnp.concatenate(pieces, 1)
-        values = apply_rows(ordered, inv[l])
+        values = apply_rows(jnp.concatenate(pieces, 1), inv[l])
         field[l] = values
         r1p[l] = product(nt, values, vh[l, 5:7].reshape(128, part), vl[l, 5:7].reshape(128, part))
-        if l % 2 == 1:
-            pair = pl.ds(l - 1, 2)
-            parts = [(r1p.at[pair], r1.at[z, pair], peer) for peer in z_peers]
-            r1_steps.append(send(parts, r1.at[three, pair]))
+        for peer in z_peers:
+            remote(send_sem.at[first + l], recv_sem.at[first + l], r1p.at[l], r1.at[z, l], peer).start()
+
+    each_leaf(solve_leaf, True)
     r1[z] = r1p[...]
 
-    raw = None
-    for l in range(leaves):
-        block = product(nt, field[l], vh[l, 0:6].reshape(384, part), vl[l, 0:6].reshape(384, part))
-        raw = block if raw is None else raw + block
+    def gram_low(l):
+        low[:, pl.ds(pl.multiple_of(128 * l, 128), 128)] = gram(l, (0, 6), (0, 2))
+
+    each_leaf(gram_low, True)
+
+    def project(l, total):
+        b_high, b_low = (t[l, 0:6].reshape(384, part) for t in (vh, vl))
+        return total + product(nt, field[l], b_high, b_low)
+
+    raw = lax.fori_loop(0, leaves, project, jnp.zeros((members, 384), f32), unroll=True)
 
     @pl.when(last_column)
     def _():
@@ -224,15 +239,28 @@
                 copy.start()
             cb[y] = core[3]
 
-    rs_step.wait_recv()
-    sum_a = rs[0] + rs[2] + rs[4] + rs[6]
-    sum_b = rs[1] + rs[3] + rs[5] + rs[7]
-    g3p[...] = low_low(sum_a[:, :, :128], sum_b[:, :, :128])
+    rsa_step.wait_recv()
+    rsb_step.wait_recv()
+    sums = [[t[j] + t[2 + j] + t[4 + j] + t[6 + j] for j in range(2)] for t in (rsa, rsb)]
+    for i in range(2):
+        g3p[2 * i : 2 * i + 2] = low_low(sums[i][0][:, :, :128], sums[i][1][:, :, :128])
+    ysp[0:2, :, :128] = sums[0][0] + sums[0][1]
+    ysp[0:2, :, 128:] = jnp.zeros((2, 8, 128), f32)
+    ysp[2:4] = sums[1][0] + sums[1][1]
     g3[:, me] = g3p[...]
-    ysp[...] = sum_a + sum_b
     ys[y] = ysp[...]
     g3_step = send([(g3p, g3.at[:, me], peer) for peer in zc_peers], g3.at[:, seven])
     ys_step = send([(ysp, ys.at[y], peer) for peer in y_peers], ys.at[three])
+    def fold_core(matrix, level, core_inverse):
+        return norm(level) * product(nn, matrix, *split(core_inverse))
+
+    quarter = [low[:, 128 * l : 128 * l + 128] for l in range(leaves)]
+    for n in range(2):
+        lanes = slice(128 * n, 128 * n + 128)
+        first_half = low_low(quarter[2 * n], quarter[2 * n + 1])
+        fold_h[:, lanes], fold_l[:, lanes] = split(fold_core(first_half, 1, core[2 * n]))
+    second = fold_core(high_high(quarter[0] + quarter[1], quarter[2] + quarter[3]), 2, core[1])
+    fold_h[:, 256:], fold_l[:, 256:] = split(second)
     g21_step.wait_recv()
     coupling = g21[0] + g21[1] + g21[2] + g21[3]
     zeros = jnp.zeros((64, 128), f32)
@@ -240,28 +268,40 @@
         [jnp.concatenate([coupling[0], zeros], 1), jnp.concatenate([zeros, coupling[1]], 1)], 0
     )
 
+    fold21 = split(
+        jnp.concatenate([fold_core(coupling[:, 128 * n : 128 * n + 128], 1, core[2 * n]) for n in range(2)], 1)
+    )
+
     for step in r1_steps:
         step.wait_recv()
     s = [r1[0, l] + r1[1, l] + r1[2, l] + r1[3, l] for l in range(leaves)]
-    s1 = [apply_rows(high_high(s[2 * n], s[2 * n + 1]), core[2 * n]) for n in range(2)]
-    p2 = low_low(s[0] + s[1], s[2] + s[3]) - apply_rows(jnp.concatenate(s1, 1), coupling)
-    s2 = apply_rows(p2, core[1])
+    p1 = [high_high(s[2 * n], s[2 * n + 1]) for n in range(2)]
+    p2 = low_low(s[0] + s[1], s[2] + s[3])
+    p2 -= product(nt, jnp.concatenate(p1, 1), *fold21)
+    r2p[...] = raw - product(nt, jnp.concatenate([*p1, p2], 1), fold_h[...], fold_l[...])
+    r2_step = send([(r2p, r2.at[me], peer) for peer in zc_peers], r2.at[seven])
+    r2[me] = r2p[...]
+
+    s1 = [apply_rows(norm(1) * p1[n], core[2 * n]) for n in range(2)]
+    s2 = apply_rows(norm(2) * p2, core[1])
     own = [
         low_low(s1[0], s2),
         jnp.where(low_lanes, turn(s1[0]), turn(s2)),
         jnp.where(low_lanes, s1[1], s2),
         high_high(s1[1], s2),
     ]
-    r2p[...] = raw - product(nt, jnp.concatenate(own, 1), q1h[...], q1l[...])
-    r2_step = send([(r2p, r2.at[me], peer) for peer in zc_peers], r2.at[seven])
-    r2[me] = r2p[...]
 
     def correct(l, coefficients, levels):
         b_high, b_low = (t[l, levels[0]:levels[1]].reshape(-1, part) for t in (uh, ul))
         return product(nn, coefficients, b_high, b_low)
 
     for l in range(leaves):
-        field[l] = field[l] - correct(l, own[l], (0, 2))
+        coefficients[l] = own[l]
+
+    def correct_low(l):
+        field[l] = field[l] - correct(l, coefficients[l], (0, 2))
+
+    each_leaf(correct_low, True)
 
     @pl.when(c == 1)
     def _():
@@ -277,9 +317,9 @@
 
     ys_step.wait_recv()
     for n in range(2):
-        g45p[4 * n : 4 * n + 4] = high_high(ys[2 * n, :, :, :128], ys[2 * n + 1, :, :, :128])
+        g45p[3 * n : 3 * n + 3] = high_high(ys[2 * n, 1:4, :, :128], ys[2 * n + 1, 1:4, :, :128])
     halves = [ys[0, 2:4, :, 128:] + ys[1, 2:4, :, 128:], ys[2, 2:4, :, 128:] + ys[3, 2:4, :, 128:]]
-    g45p[8:10] = low_low(halves[0], halves[1])
+    g45p[6:8] = low_low(halves[0], halves[1])
     xsp[...] = halves[0][1] + halves[1][1]
     g45[:, me] = g45p[...]
     xs[x] = xsp[...]
@@ -292,11 +332,12 @@
     def _():
         third.wait_recv()
 
+    fold3 = split(fold_core(g3[...].reshape(256, 128), 3, c3[...]))
     r2_step.wait_recv()
     p_a = r2[0] + r2[2] + r2[4] + r2[6]
     p_b = r2[1] + r2[3] + r2[5] + r2[7]
-    s3 = apply_rows(low_low(p_a[:, 256:], p_b[:, 256:]), c3[...])
-    r3p[...] = p_a[:, :256] + p_b[:, :256] - apply_rows(s3, g3[...].reshape(256, 128))
+    p3 = low_low(p_a[:, 256:], p_b[:, 256:])
+    r3p[...] = p_a[:, :256] + p_b[:, :256] - product(nt, p3, *fold3)
     r3_step = send([(r3p, r3.at[y], peer) for peer in y_peers], r3.at[three])
     r3[y] = r3p[...]
 
@@ -311,24 +352,37 @@
         to_sibling.wait_recv()
 
     g45_step.wait_recv()
+    fold5 = fold_core(g45[6:8].reshape(128, 128), 5, cb[1])
+    fold45 = []
+    for n in range(2):
+        fold4 = fold_core(g45[3 * n : 3 * n + 3].reshape(192, 128), 4, cb[2 * n])
+        half = fold5[:, 64 * n : 64 * n + 64]
+        fold45.append(fold4[64:] - product(nn, half, *split(fold4[:64])))
+    fold45 = split(jnp.concatenate([*fold45, fold5], 1))
     r3_step.wait_recv()
-    s4, below = [], []
-    for n in range(2):
-        p4 = low_low(r3[2 * n, :, :128], r3[2 * n + 1, :, :128])
-        s4.append(apply_rows(p4, cb[2 * n]))
-        below.append(r3[2 * n] + r3[2 * n + 1] - apply_rows(s4[n], g45[4 * n : 4 * n + 4].reshape(256, 128)))
-    s5 = apply_rows(high_high(below[0][:, :128], below[1][:, :128]), cb[1])
-    r4p[...] = below[0][:, 128:] + below[1][:, 128:] - apply_rows(s5, g45[8:10].reshape(128, 128))
+    p4 = [low_low(r3[2 * n, :, :128], r3[2 * n + 1, :, :128]) for n in range(2)]
+    pair = [r3[2 * n] + r3[2 * n + 1] for n in range(2)]
+    p5 = high_high(pair[0][:, :128], pair[1][:, :128])
+    r4p[...] = (
+        pair[0][:, 128:] + pair[1][:, 128:] - product(nt, jnp.concatenate([*p4, p5], 1), *fold45)
+    )
     r4_step = send([(r4p, r4.at[x], peer) for peer in x_peers], r4.at[three])
     r4[x] = r4p[...]
 
+    s3 = apply_rows(norm(3) * p3, c3[...])
+    s4 = [apply_rows(norm(4) * p4[n], cb[2 * n]) for n in range(2)]
+    below = [apply_rows(s4[n], g45[3 * n].reshape(64, 128)) for n in range(2)]
+    s5 = apply_rows(norm(5) * (p5 - jnp.concatenate(below, 1)), cb[1])
     own3 = jnp.where(c == 0, s3, turn(s3))
     own4 = jnp.where(y < 2, s4[0], s4[1])
     own4 = jnp.where(lax.rem(y, 2) == 1, own4, turn(own4))
     own5 = jnp.where(y < 2, s5, turn(s5))
     own34 = jnp.where(low_lanes, own3, own4)
-    for l in range(leaves):
+
+    def correct_middle(l):
         field[l] = field[l] - correct(l, own34, (2, 4)) - correct(l, own5[:, :64], (4, 5))
+
+    each_leaf(correct_middle, True)
 
     g6_step.wait_recv()
     coupling = jnp.concatenate(
@@ -338,16 +392,26 @@
         ],
         0,
     )
+    c7 = norm(7) * jnp.where(x < 2, cb[4, :64], cb[4, 64:])
+    c6 = jnp.where(x < 2, cb[3], cb[5])
+    c6 = norm(6) * jnp.where(lax.rem(x, 2) == 0, c6[:64], c6[64:])
+    fold67 = []
+    for n in range(2):
+        lanes = slice(128 * n, 128 * n + 128)
+        below7 = fold_core(product(nn, c7, *split(coupling[:, lanes])), 6, cb[3 + 2 * n])
+        here = jnp.where(lax.div(x, 2) == n, c6, zeros)
+        fold67.append(jnp.concatenate([here, -below7], 0))
+    fold67.append(jnp.concatenate([zeros, c7], 0))
+    fold67 = split(jnp.concatenate(fold67, 1))
     r4_step.wait_recv()
-    s6 = [apply_rows(low_low(r4[2 * n], r4[2 * n + 1]), cb[3 + 2 * n]) for n in range(2)]
-    p7 = high_high(r4[0] + r4[1], r4[2] + r4[3]) - apply_rows(jnp.concatenate(s6, 1), coupling)
-    s7 = apply_rows(p7, cb[4])
-    own6 = jnp.where(x < 2, s6[0], s6[1])
-    own6 = jnp.where(lax.rem(x, 2) == 0, own6, turn(own6))
-    own7 = jnp.where(x < 2, turn(s7), s7)
-    own67 = jnp.where(low_lanes, own6, own7)
-    for l in range(leaves):
+    p6 = [low_low(r4[2 * n], r4[2 * n + 1]) for n in range(2)]
+    p7 = high_high(r4[0] + r4[1], r4[2] + r4[3])
+    own67 = product(nt, jnp.concatenate([*p6, p7], 1), *fold67)
+
+    def correct_high(l):
         out[l] = field[l] - correct(l, own67, (5, 7))
+
+    each_leaf(correct_high, True)
 
     for step in steps:
         step.wait_send()
@@ -376,7 +440,7 @@
     vmem = pltpu.VMEM
     scratch = [
         vmem((4, leaves, members, part), f32),
-        vmem((leaves, size), jnp.int32),
+        vmem((leaves, 1, size), jnp.int32),
         vmem((leaves, part, size), f32),
         vmem((leaves, 7, 64, part), f32),
         vmem((leaves, 7, 64, part), f32),
@@ -385,17 +449,19 @@
         vmem((leaves, 7, 64, part), bf16),
         vmem((leaves, 7, 64, part), bf16),
         vmem((leaves, 7, 64, part), bf16),
+        vmem((384, 384), bf16),
+        vmem((384, 384), bf16),
         vmem((384, 512), f32),
-        vmem((384, 512), bf16),
-        vmem((384, 512), bf16),
-        vmem((4, 8, 8, 256), f32),
+        vmem((2, 8, 8, 128), f32),
+        vmem((2, 8, 8, 256), f32),
         vmem((2, 64, 128), f32),
         vmem((4, 2, 64, 128), f32),
-        vmem((8, 4, 8, 256), f32),
+        vmem((8, 2, 8, 128), f32),
+        vmem((8, 2, 8, 256), f32),
         vmem((4, 8, 8, 128), f32),
         vmem((4, 4, 8, 256), f32),
-        vmem((10, 8, 128), f32),
-        vmem((10, 8, 8, 128), f32),
+        vmem((8, 8, 128), f32),
+        vmem((8, 8, 8, 128), f32),
         vmem((4, 8, 128), f32),
         vmem((2, 8, 128), f32),
         vmem((2, 8, 8, 128), f32),
@@ -406,6 +472,7 @@
         vmem((6, 128, 128), f32),
         vmem((128, 128), f32),
         vmem((leaves, members, part), f32),
+        vmem((leaves, members, 128), f32),
         vmem((leaves, members, 128), f32),
         vmem((4, leaves, members, 128), f32),
         vmem((members, 384), f32),

time: 36.7 us -> 34.7 us (0.946)
  Pallas kernels: 35.1 us -> 33.1 us
    pallas_call x1, Pallas kernels: 35.1 us -> 33.1 us  [per_device(): pl.pallas_call(kernel, out_shape=jax.ShapeDtypeStruct((leaves, members, p...]
where the time goes in v4:
time: 34.7 us; the launch traced here: 34.5 us
  Pallas kernels  33.1 us (95%)
  local copies, waits for them, and re-layouts  1.39 us (4%)
    pallas_call x1, Pallas kernels, per_device(): pl.pallas_call(kernel, out_shape=jax.ShapeDtypeStruct((leaves, members, p...  33.1 us
    unnamed x2, local copies, waits for them, and re-layouts  0.72 us

profile of v4, /device:TPU:1, one launch (start us, length us, event | category | flops | bytes accessed | tf_op | source)
XLA Modules:
  0.0 34.5 jit_solution(12331183407141604298)
XLA Ops:
  0.0 0.0 copy-start
  0.0 0.7 %copy-done = s32[4,1024]{1,0:T(4,128)S(1)} copy-done((s32[4,1024]{1,0:T(4,128)S(1)}, s32[4,1024]{1,0:T(4,128)}, u32[]{:S(2)}) %copy-start) | copy-done | bytes 16408
  0.7 33.1 %shard_map.64 = f32[4,16,256]{2,1,0:T(8,128)S(1)} custom-call(f32[16,4,256]{2,1,0:T(4,128)} %right.1, s32[4,1024]{1,0:T(4,128)S(1)} %copy-done, f32[4,256,1024]{2,1,0:T(8,128)} %inverse.1, f32[7,64,4,256]{3,2,1,0:T(4,128)} %left.1, f32[7,64,4,256]{3,2,1,0:T(4,128)} %column.1, f32[4,128,128]{2,1,0:T(8,128)} %cores.1), custom_call_target="tpu_custom_call" | custom-call | tf_op jit(solution)/shard_map/pallas_call | solution.py:490
  33.9 0.7 %copy.7 = f32[16,4,256]{2,1,0:T(4,128)} copy(f32[16,4,256]{2,0,1:T(8,128)S(1)} %bitcast.1) | data formatting | bytes 131072 | tf_op jit(solution)/shard_map/transpose | solution.py:500
Async XLA Ops:
  0.0 0.7 %copy-start = (s32[4,1024]{1,0:T(4,128)S(1)}, s32[4,1024]{1,0:T(4,128)}, u32[]{:S(2)}) copy-start(s32[4,1024]{1,0:T(4,128)} %order.1) | copy-start | bytes 49156

commit v5 on v4

--- a/solution.py
+++ b/solution.py
@@ -174,6 +174,8 @@
     q3b[...] = total[128:].reshape(2, 8, 8, 256)
     rsa[me] = q3a[:, me]
     rsb[me] = q3b[:, me]
+    for step in rhs_steps:
+        step.wait_send()
     zc_pairs = list(zip(zc_index, zc_peers, strict=True))
     rsa_step = send([(q3a.at[:, i], rsa.at[me], peer) for i, peer in zc_pairs], rsa.at[seven])
     rsb_step = send([(q3b.at[:, i], rsb.at[me], peer) for i, peer in zc_pairs], rsb.at[seven])
@@ -282,39 +284,6 @@
     r2_step = send([(r2p, r2.at[me], peer) for peer in zc_peers], r2.at[seven])
     r2[me] = r2p[...]
 
-    s1 = [apply_rows(norm(1) * p1[n], core[2 * n]) for n in range(2)]
-    s2 = apply_rows(norm(2) * p2, core[1])
-    own = [
-        low_low(s1[0], s2),
-        jnp.where(low_lanes, turn(s1[0]), turn(s2)),
-        jnp.where(low_lanes, s1[1], s2),
-        high_high(s1[1], s2),
-    ]
-
-    def correct(l, coefficients, levels):
-        b_high, b_low = (t[l, levels[0]:levels[1]].reshape(-1, part) for t in (uh, ul))
-        return product(nn, coefficients, b_high, b_low)
-
-    for l in range(leaves):
-        coefficients[l] = own[l]
-
-    def correct_low(l):
-        field[l] = field[l] - correct(l, coefficients[l], (0, 2))
-
-    each_leaf(correct_low, True)
-
-    @pl.when(c == 1)
-    def _():
-        @pl.when(y == 3)
-        def _():
-            core_wait(1, cb.at[three]).wait_recv()
-
-        @pl.when(y < 3)
-        def _():
-            core_wait(1, cb.at[pl.ds(0, 5)]).wait_recv()
-
-        to_sibling.start()
-
     ys_step.wait_recv()
     for n in range(2):
         g45p[3 * n : 3 * n + 3] = high_high(ys[2 * n, 1:4, :, :128], ys[2 * n + 1, 1:4, :, :128])
@@ -325,6 +294,39 @@
     xs[x] = xsp[...]
     xs_step = send([(xsp, xs.at[x], peer) for peer in x_peers], xs.at[three])
     g45_step = send([(g45p, g45.at[:, me], peer) for peer in zc_peers], g45.at[:, seven])
+
+    s1 = [apply_rows(norm(1) * p1[n], core[2 * n]) for n in range(2)]
+    s2 = apply_rows(norm(2) * p2, core[1])
+    own = [
+        low_low(s1[0], s2),
+        jnp.where(low_lanes, turn(s1[0]), turn(s2)),
+        jnp.where(low_lanes, s1[1], s2),
+        high_high(s1[1], s2),
+    ]
+
+    def correct(l, coefficients, levels):
+        b_high, b_low = (t[l, levels[0]:levels[1]].reshape(-1, part) for t in (uh, ul))
+        return product(nn, coefficients, b_high, b_low)
+
+    for l in range(leaves):
+        coefficients[l] = own[l]
+
+    def correct_low(l):
+        field[l] = field[l] - correct(l, coefficients[l], (0, 2))
+
+    each_leaf(correct_low, True)
+
+    @pl.when(c == 1)
+    def _():
+        @pl.when(y == 3)
+        def _():
+            core_wait(1, cb.at[three]).wait_recv()
+
+        @pl.when(y < 3)
+        def _():
+            core_wait(1, cb.at[pl.ds(0, 5)]).wait_recv()
+
+        to_sibling.start()
 
     g3_step.wait_recv()
 
@@ -413,7 +415,7 @@
 
     each_leaf(correct_high, True)
 
-    for step in steps:
+    for step in steps[leaves:]:
         step.wait_send()
 
     @pl.when(last_column)

time: 34.7 us -> 34.4 us (level)
  no operation moved by 1% of the time
where the time goes in v5:
time: 34.4 us; the launch traced here: 34.3 us
  Pallas kernels  32.9 us (96%)
  local copies, waits for them, and re-layouts  1.39 us (4%)
    pallas_call x1, Pallas kernels, per_device(): pl.pallas_call(kernel, out_shape=jax.ShapeDtypeStruct((leaves, members, p...  32.9 us
    unnamed x2, local copies, waits for them, and re-layouts  0.72 us

profile of v5, /device:TPU:1, one launch (start us, length us, event | category | flops | bytes accessed | tf_op | source)
XLA Modules:
  0.0 34.3 jit_solution(11392978201343153799)
XLA Ops:
  0.0 0.0 copy-start
  0.0 0.7 %copy-done = s32[4,1024]{1,0:T(4,128)S(1)} copy-done((s32[4,1024]{1,0:T(4,128)S(1)}, s32[4,1024]{1,0:T(4,128)}, u32[]{:S(2)}) %copy-start) | copy-done | bytes 16408
  0.7 32.9 %shard_map.64 = f32[4,16,256]{2,1,0:T(8,128)S(1)} custom-call(f32[16,4,256]{2,1,0:T(4,128)} %right.1, s32[4,1024]{1,0:T(4,128)S(1)} %copy-done, f32[4,256,1024]{2,1,0:T(8,128)} %inverse.1, f32[7,64,4,256]{3,2,1,0:T(4,128)} %left.1, f32[7,64,4,256]{3,2,1,0:T(4,128)} %column.1, f32[4,128,128]{2,1,0:T(8,128)} %cores.1), custom_call_target="tpu_custom_call" | custom-call | tf_op jit(solution)/shard_map/pallas_call | solution.py:492
  33.6 0.7 %copy.7 = f32[16,4,256]{2,1,0:T(4,128)} copy(f32[16,4,256]{2,0,1:T(8,128)S(1)} %bitcast.1) | data formatting | bytes 131072 | tf_op jit(solution)/shard_map/transpose | solution.py:502
Async XLA Ops:
  0.0 0.7 %copy-start = (s32[4,1024]{1,0:T(4,128)S(1)}, s32[4,1024]{1,0:T(4,128)}, u32[]{:S(2)}) copy-start(s32[4,1024]{1,0:T(4,128)} %order.1) | copy-start | bytes 49156
